TPU v7x, 256 devices: a whole 4x4x8 slice. The times are simulated.
256 devices in a mesh: section: 4 (over z_hi), dp: 64 (over z_lo, x, y, core).
Axes of the slice: x: 4, y: 4, z: 8 (z_hi: 4, z_lo: 2; z = z_hi * 2 + z_lo), core: 2. Of those that a mesh axis runs over, the one named last changes fastest.
Arguments:
- acts: bfloat16 [4, 2, 4096, 4096], P('section', None, 'dp'), may hold values from -16 to 16
- cotangent: bfloat16 [2, 4096, 4096], P(None, 'dp'), may hold values from -16 to 16
- perm_up: int32 [4, 4096], P('section'), may hold values from 0 to 4095, each once within a row
- perm_dn: int32 [4, 4096], P('section'), may hold values from 0 to 4095, each once within a row
- left_up: bfloat16 [4, 4096, 256], P('section', 'dp'), may hold values from -0.375 to 0.375
- right_up: bfloat16 [4, 4096, 256], P('section', 'dp'), may hold values from -0.75 to 0.75
- right_dn: bfloat16 [4, 4096, 256], P('section', 'dp'), may hold values from -0.375 to 0.375
- left_dn: bfloat16 [4, 4096, 256], P('section', 'dp'), may hold values from -0.375 to 0.375
Outputs:
- input_grads: bfloat16 [4, 2, 4096, 4096], P('section', None, 'dp')
- grad_left_up: float32 [4, 4096, 256], P('section', 'dp')
- grad_right_up: float32 [4, 4096, 256], P('section', 'dp')
- grad_right_dn: float32 [4, 4096, 256], P('section', 'dp')
- grad_left_dn: float32 [4, 4096, 256], P('section', 'dp')
Inputs may be any that keep to these rules, and one draw needn't show every extreme that they name: Every row of perm_up names each of 0 to 4095 once. Every row of perm_dn names each of 0 to 4095 once.
All inputs are finite; a program needn't handle non-finite values.
Results may differ from a plain program's by a relative error of at most 0.028.
Values may be sent and summed in bfloat16 or wider, within the bound.
No kernel may reach another device: no remote copies, remote signals or barrier semaphores. Data moves between devices by JAX's collectives and lax.ppermute only.
A program may use at most 128 MiB of HBM per device.

v0:
```python
import jax
import jax.numpy as jnp
from jax import lax
from jax.sharding import PartitionSpec as P

FF = 16384


epsilon = 1e-06


def from_behind(block, axis, distance):
    devices = range(lax.axis_size(axis))
    route = [(i - distance, i) for i in devices if i - distance in devices]
    return lax.ppermute(block, axis, route)


def inverse_of(permute):
    count = permute.shape[0]
    return jnp.zeros((count,), jnp.int32).at[permute].set(jnp.arange(count, dtype=jnp.int32))


def contract(form, first, second):
    return jnp.einsum(form, first, second, preferred_element_type=jnp.float32)


def forward_part(rows_in, weights, tables):
    left_first, right_first, right_second, left_second = weights
    perm_first, perm_second, inv_first, inv_second = tables
    nblock, width, _ = left_first.shape
    nhidden, narrow, _ = right_first.shape
    count = rows_in.shape[0]
    in_float = rows_in.T.astype(jnp.float32)
    scaling = lax.rsqrt(jnp.mean(in_float * in_float, axis=0, keepdims=True) + epsilon)
    normf = in_float * scaling
    normed = normf.astype(jnp.bfloat16).reshape(nblock, width, count)
    up_mid = contract("jio,jit->jot", left_first, normed).astype(jnp.bfloat16).reshape(-1, count)
    shuffled = jnp.take(up_mid, perm_first, axis=0).reshape(nhidden, narrow, count)
    hidden = contract("kio,kit->kot", right_first, shuffled)
    squashed = jax.nn.sigmoid(hidden)
    active = (hidden * squashed).astype(jnp.bfloat16)
    slope = (squashed * (1.0 + hidden * (1.0 - squashed))).astype(jnp.bfloat16)
    down_mid = (
        contract("kio,kot->kit", right_second, active).astype(jnp.bfloat16).reshape(-1, count)
    )
    placed = jnp.take(down_mid, perm_second, axis=0).reshape(nblock, width, count)
    return (scaling, normf, normed, shuffled, active, slope, placed)


def backward_part(grad_rows, scaling, normf, slope, weights, tables):
    left_first, right_first, right_second, left_second = weights
    perm_first, perm_second, inv_first, inv_second = tables
    nblock, width, _ = left_first.shape
    nhidden, narrow, _ = right_first.shape
    count = grad_rows.shape[0]
    grad_col = grad_rows.T
    grad_out = grad_col.reshape(nblock, width, count)
    grad_placed = (
        contract("jio,jot->jit", left_second, grad_out).astype(jnp.bfloat16).reshape(-1, count)
    )
    grad_down = jnp.take(grad_placed, inv_second, axis=0).reshape(nhidden, narrow, count)
    grad_active = contract("kio,kit->kot", right_second, grad_down).astype(jnp.bfloat16)
    grad_hidden = (grad_active.astype(jnp.float32) * slope.astype(jnp.float32)).astype(jnp.bfloat16)
    grad_shuffled = (
        contract("kio,kot->kit", right_first, grad_hidden).astype(jnp.bfloat16).reshape(-1, count)
    )
    grad_upmid = jnp.take(grad_shuffled, inv_first, axis=0).reshape(nblock, width, count)
    grad_norm = contract("jio,jot->jit", left_first, grad_upmid).reshape(-1, count)
    inner = jnp.mean(grad_norm * normf, axis=0, keepdims=True)
    grad_input = grad_col.astype(jnp.float32) + scaling * (grad_norm - normf * inner)
    return (grad_input.astype(jnp.bfloat16).T, grad_out, grad_down, grad_hidden, grad_upmid)


def shards(acts, cotangent, perm_up, perm_dn, left_up, right_up, right_dn, left_dn):
    gathered = (
        lax.all_gather(left_up, "dp", axis=1, tiled=True),
        lax.all_gather(right_up, "dp", axis=1, tiled=True),
        lax.all_gather(right_dn, "dp", axis=1, tiled=True),
        lax.all_gather(left_dn, "dp", axis=1, tiled=True),
    )
    model_width = gathered[0].shape[1]
    width = gathered[0].shape[2]
    nblock = model_width // width
    nhidden = FF // width
    narrow = model_width // nhidden
    weights = (
        gathered[0][0].reshape(nblock, width, width),
        gathered[1][0].reshape(nhidden, narrow, width),
        gathered[2][0].reshape(nhidden, narrow, width),
        gathered[3][0].reshape(nblock, width, width),
    )
    tables = (perm_up[0], perm_dn[0], inverse_of(perm_up[0]), inverse_of(perm_dn[0]))
    section_count = lax.axis_size("section")
    section_index = lax.axis_index("section")
    final_section = section_count - 1
    micro_count = acts.shape[1]
    tok_rows = acts.shape[2]
    local_acts = acts[0]
    all_rows = micro_count * tok_rows
    scaling, normf, normed, shuffled, active, slope, placed = forward_part(
        local_acts.reshape(all_rows, model_width), weights, tables
    )
    results = jnp.zeros_like(local_acts)
    incoming = jnp.zeros_like(local_acts)

    def whole_section(operands):
        grad_all, kept = operands
        grad_input = backward_part(
            grad_all.reshape(all_rows, model_width), scaling, normf, slope, weights, tables
        )[0]
        return grad_input.reshape(micro_count, tok_rows, model_width)

    def hold_section(operands):
        return operands[1]

    for step_index in range(section_count):
        grad_all = jnp.where(section_index == final_section, cotangent, incoming)
        results = lax.cond(
            section_index == final_section - step_index,
            whole_section,
            hold_section,
            (grad_all, results),
        )
        if step_index + 1 < section_count:
            incoming = from_behind(results, "section", -1)
    grad_all = jnp.where(section_index == final_section, cotangent, incoming)
    unused, grad_out, grad_down, grad_hidden, grad_upmid = backward_part(
        grad_all.reshape(all_rows, model_width), scaling, normf, slope, weights, tables
    )
    totals = (
        contract("jit,jot->jio", normed, grad_upmid).reshape(-1, width),
        contract("kit,kot->kio", shuffled, grad_hidden).reshape(-1, width),
        contract("kit,kot->kio", grad_down, active).reshape(-1, width),
        contract("jit,jot->jio", placed, grad_out).reshape(-1, width),
    )
    owned = (
        lax.psum_scatter(totals[0], "dp", scatter_dimension=0, tiled=True),
        lax.psum_scatter(totals[1], "dp", scatter_dimension=0, tiled=True),
        lax.psum_scatter(totals[2], "dp", scatter_dimension=0, tiled=True),
        lax.psum_scatter(totals[3], "dp", scatter_dimension=0, tiled=True),
    )
    return (results[None], owned[0][None], owned[1][None], owned[2][None], owned[3][None])


def solution(mesh):
    return jax.shard_map(
        shards,
        mesh=mesh,
        in_specs=(
            P("section", None, "dp", None),
            P(None, "dp", None),
            P("section", None),
            P("section", None),
            P("section", "dp", None),
            P("section", "dp", None),
            P("section", "dp", None),
            P("section", "dp", None),
        ),
        out_specs=(
            P("section", None, "dp", None),
            P("section", "dp", None),
            P("section", "dp", None),
            P("section", "dp", None),
            P("section", "dp", None),
        ),
        check_vma=False,
    )
```

profile of v0, /device:TPU:6, one launch (start us, length us, event | category | flops | bytes accessed | tf_op | source)
XLA Modules:
  0.0 1939.2 jit_solution(7350091349072340213)
XLA Ops:
  7.2 0.7 all-gather.9.cloned.1.call-update
  7.9 0.7 all-gather.11.cloned.1.call-update
  8.7 0.7 all-gather.7.cloned.1.call-update
  9.4 0.5 all-gather.5.cloned.1.call-update
  10.0 1.5 fusion.61
  11.5 2.6 fusion.62
  14.1 1.6 copy.82
  15.8 15.5 scatter_custom_fusion
  31.4 15.5 scatter_custom_fusion.1
  46.9 70.4 %all-gather.9.cloned.1.call-done = bf16[1,4096,256]{2,1,0:T(8,128)(2,1)} async-done(((bf16[1,64,256]{2,1,0:T(8,128)(2,1)}), bf16[1,4096,256]{2,1,0:T(8,128)(2,1)}) %all-gather.9.cloned.1.call-update) | async-done | bytes 2097168 | tf_op jit(solution)/shard_map/all_gather | solution.py:76
  117.3 3.1 fusion.63
  120.4 1.6 copy.60
  122.0 15.0 gather_fusion.8
  137.1 4.2 broadcast_select_fusion.14
  141.3 82.3 %all-gather.11.cloned.1.call-done = bf16[1,4096,256]{2,1,0:T(8,128)(2,1)} async-done(((bf16[1,64,256]{2,1,0:T(8,128)(2,1)}), bf16[1,4096,256]{2,1,0:T(8,128)(2,1)}) %all-gather.11.cloned.1.call-update) | async-done | bytes 2097168 | tf_op jit(solution)/shard_map/all_gather | solution.py:77
  223.7 9.1 fusion.60
  232.7 97.3 %all-gather.7.cloned.1.call-done = bf16[1,4096,256]{2,1,0:T(8,128)(2,1)} async-done(((bf16[1,64,256]{2,1,0:T(8,128)(2,1)}), bf16[1,4096,256]{2,1,0:T(8,128)(2,1)}) %all-gather.7.cloned.1.call-update) | async-done | bytes 2097168 | tf_op jit(solution)/shard_map/all_gather | solution.py:78
  330.0 106.2 %all-gather.5.cloned.1.call-done = bf16[1,4096,256]{2,1,0:T(8,128)(2,1)} async-done(((bf16[1,64,256]{2,1,0:T(8,128)(2,1)}), bf16[1,4096,256]{2,1,0:T(8,128)(2,1)}) %all-gather.5.cloned.1.call-update) | async-done | bytes 2097168 | tf_op jit(solution)/shard_map/all_gather | solution.py:79
  436.2 1.2 conditional.4
  436.2 1.1 broadcast.100
  437.5 1.3 collective-permute-start
  438.8 49.6 %collective-permute-done = bf16[2,64,4096]{2,1,0:T(8,128)(2,1)S(1)} collective-permute-done((bf16[2,64,4096]{2,1,0:T(8,128)(2,1)}, bf16[2,64,4096]{2,1,0:T(8,128)(2,1)S(1)}, u32[]{:S(2)}, u32[]{:S(2)}) %collective-permute-start) | collective-permute-done | bytes 1048608 | tf_op jit(solution)/shard_map/ppermute | solution.py:15
  488.5 1.3 collective-permute-start.1
  489.8 46.6 %collective-permute-done.1 = bf16[2,64,4096]{2,1,0:T(8,128)(2,1)S(1)} collective-permute-done((bf16[2,64,4096]{2,1,0:T(8,128)(2,1)}, bf16[2,64,4096]{2,1,0:T(8,128)(2,1)S(1)}, u32[]{:S(2)}, u32[]{:S(2)}) %collective-permute-start.1) | collective-permute-done | bytes 1048608 | tf_op jit(solution)/shard_map/ppermute | solution.py:15
  536.6 1.3 collective-permute-start.2
  538.0 218.7 %collective-permute-done.2 = bf16[2,64,4096]{2,1,0:T(8,128)(2,1)S(1)} collective-permute-done((bf16[2,64,4096]{2,1,0:T(8,128)(2,1)}, bf16[2,64,4096]{2,1,0:T(8,128)(2,1)S(1)}, u32[]{:S(2)}, u32[]{:S(2)}) %collective-permute-start.2) | collective-permute-done | bytes 1048608 | tf_op jit(solution)/shard_map/ppermute | solution.py:15
  756.8 1.4 copy.83
  758.2 3.7 fusion.64
  761.9 1.6 copy.66
  763.5 15.0 gather_fusion.9
  778.5 3.4 broadcast_select_fusion.13
  781.9 5.3 fusion.77
  787.3 0.5 reduce-scatter.11.cloned.1.call-start
  787.8 4.4 convolution_convert_fusion.4
  792.3 15.0 gather_fusion.11
  807.3 3.5 broadcast_select_fusion.11
  810.8 2.7 fusion.78
  813.6 1.1 copy-done.18
  814.8 4.2 fusion.53
  819.0 3.1 fusion.76
  822.3 4.5 convolution_convert_fusion.5
  826.8 15.0 gather_fusion.10
  841.8 3.5 broadcast_select_fusion.12
  845.3 2.7 fusion.75
  848.0 1.2 copy-done.10
  849.2 70.5 %conditional.7 = (bf16[1,2,64,4096]{3,2,1,0:T(8,128)(2,1)}) conditional(s32[]{:T(128)} %convert_element_type.192, bf16[2,64,4096]{2,1,0:T(8,128)(2,1)} %get-tuple-element.297, (bf16[2,64,4096]{2,1,0:T(8,128)(2,1)S(1)}, f32[1,128]{1,0:T(1,128)S(1)}, bf16[16,256,256]{2,1,0:T(8,128)(2,1)}, s32[4096]{0:T(1024)S(1)}, bf16[64,64,256]{2,1,0:T(8,128)(2,1)}, ...), branch_computations={%region_12.14_spmd, %region_13.16_spmd} | conditional | flops 1090600960 | bytes 78793312 | solution.py:118
  849.4 1.3 copy.81
  850.7 2.6 convolution_convert_fusion.3
  853.3 15.0 gather_fusion.6
  868.3 4.2 broadcast_select_fusion.10
  872.6 6.4 copy.64
  879.0 6.1 fusion.48
  885.1 15.0 gather_fusion.7
  900.1 3.5 broadcast_select_fusion.9
  903.7 2.2 convolution_bitcast_fusion.3
  905.9 2.9 copy.56
  908.8 1.9 copy.57
  910.7 2.8 multiply_reduce_fusion.3
  913.5 3.1 copy.58
  916.6 3.1 add_convert_fusion.3
  919.7 138.0 %reduce-scatter.9.cloned.1.call-done = f32[64,256]{1,0:T(8,128)} async-done(((f32[4096,256]{1,0:T(8,128)}), f32[64,256]{1,0:T(8,128)}) %reduce-scatter.9.cloned.1.call-update) | async-done | bytes 65552 | tf_op jit(solution)/shard_map/reduce_scatter | solution.py:139
  1057.7 291.7 %reduce-scatter.11.cloned.1.call-done = f32[64,256]{1,0:T(8,128)} async-done(((f32[4096,256]{1,0:T(8,128)}), f32[64,256]{1,0:T(8,128)}) %reduce-scatter.11.cloned.1.call-update) | async-done | bytes 65552 | tf_op jit(solution)/shard_map/reduce_scatter | solution.py:140
  1349.5 291.7 %reduce-scatter.7.cloned.1.call-done = f32[64,256]{1,0:T(8,128)} async-done(((f32[4096,256]{1,0:T(8,128)}), f32[64,256]{1,0:T(8,128)}) %reduce-scatter.7.cloned.1.call-update) | async-done | bytes 65552 | tf_op jit(solution)/shard_map/reduce_scatter | solution.py:138
  1641.2 291.0 %reduce-scatter.5.cloned.1.call-done = f32[64,256]{1,0:T(8,128)} async-done(((f32[4096,256]{1,0:T(8,128)}), f32[64,256]{1,0:T(8,128)}) %reduce-scatter.5.cloned.1.call-update) | async-done | bytes 65552 | tf_op jit(solution)/shard_map/reduce_scatter | solution.py:137
  (58 shorter events, 1.2 us)
Async XLA Ops:
  7.2 110.2 %all-gather.9.cloned.1.call-start = ((), (), s32[]{:S(2)}) async-start(), calls=%async_computation.6 | async-start | bytes 2129920 | tf_op jit(solution)/shard_map/all_gather | solution.py:76
  7.9 215.8 %all-gather.11.cloned.1.call-start = ((), (), s32[]{:S(2)}) async-start(), calls=%async_computation.7 | async-start | bytes 2129920 | tf_op jit(solution)/shard_map/all_gather | solution.py:77
  8.6 321.4 %all-gather.7.cloned.1.call-start = ((), (), s32[]{:S(2)}) async-start(), calls=%async_computation.5 | async-start | bytes 2129920 | tf_op jit(solution)/shard_map/all_gather | solution.py:78
  9.4 426.8 %all-gather.5.cloned.1.call-start = ((), (), s32[]{:S(2)}) async-start(), calls=%async_computation.4 | async-start | bytes 2129920 | tf_op jit(solution)/shard_map/all_gather | solution.py:79
  10.0 1047.8 %reduce-scatter.9.cloned.1.call-start = ((), (), s32[]{:S(2)}) async-start(), calls=%async_computation.10 | async-start | bytes 4259840 | tf_op jit(solution)/shard_map/reduce_scatter | solution.py:139
  11.5 2.6 copy-start.26
  14.1 17.2 copy-start.25
  15.8 101.6 %copy-start.15 = (bf16[4096,128]{1,0:T(8,128)(2,1)}, bf16[4096,128]{1,0:T(8,128)(2,1)S(1)}, u32[]{:S(2)}) copy-start(bf16[4096,128]{1,0:T(8,128)(2,1)S(1)} %copy.82) | copy-start | bytes 3145732
  223.7 212.6 %copy-start.8 = (bf16[2,64,4096]{2,1,0:T(8,128)(2,1)S(1)}, bf16[2,64,4096]{2,1,0:T(8,128)(2,1)}, u32[]{:S(2)}) copy-start(bf16[2,64,4096]{2,1,0:T(8,128)(2,1)} %param.19) | copy-start | bytes 3145732
  437.5 50.9 %collective-permute-start = (bf16[2,64,4096]{2,1,0:T(8,128)(2,1)}, bf16[2,64,4096]{2,1,0:T(8,128)(2,1)S(1)}, u32[]{:S(2)}, u32[]{:S(2)}) collective-permute-start(bf16[2,64,4096]{2,1,0:T(8,128)(2,1)} %get-tuple-element.295), channel_id=1, source_target_pairs={{64,0},{128,64},{192,128},{65,1},{129,65},{193,129},{66,2},{130,66... | collective-permute-start | bytes 3145736 | tf_op jit(solution)/shard_map/ppermute | solution.py:15
  488.5 47.9 %collective-permute-start.1 = (bf16[2,64,4096]{2,1,0:T(8,128)(2,1)}, bf16[2,64,4096]{2,1,0:T(8,128)(2,1)S(1)}, u32[]{:S(2)}, u32[]{:S(2)}) collective-permute-start(bf16[2,64,4096]{2,1,0:T(8,128)(2,1)} %get-tuple-element.296), channel_id=1, source_target_pairs={{64,0},{128,64},{192,128},{65,1},{129,65},{193,129},{66,2},{130,66... | collective-permute-start | bytes 3145736 | tf_op jit(solution)/shard_map/ppermute | solution.py:15
  536.6 220.0 %collective-permute-start.2 = (bf16[2,64,4096]{2,1,0:T(8,128)(2,1)}, bf16[2,64,4096]{2,1,0:T(8,128)(2,1)S(1)}, u32[]{:S(2)}, u32[]{:S(2)}) collective-permute-start(bf16[2,64,4096]{2,1,0:T(8,128)(2,1)} %get-tuple-element.297), channel_id=1, source_target_pairs={{64,0},{128,64},{192,128},{65,1},{129,65},{193,129},{66,2},{130,66... | collective-permute-start | bytes 3145736 | tf_op jit(solution)/shard_map/ppermute | solution.py:15
  756.8 1.4 copy-start.9
  781.9 5.3 copy-start.17
  787.3 562.2 %reduce-scatter.11.cloned.1.call-start = ((), (), s32[]{:S(2)}) async-start(), calls=%async_computation.11 | async-start | bytes 4259840 | tf_op jit(solution)/shard_map/reduce_scatter | solution.py:140
  807.3 3.5 copy-start.23
  813.5 1.2 copy-start.18
  813.6 827.6 %reduce-scatter.7.cloned.1.call-start = ((), (), s32[]{:S(2)}) async-start(), calls=%async_computation.9 | async-start | bytes 4259840 | tf_op jit(solution)/shard_map/reduce_scatter | solution.py:138
  814.8 4.2 copy-start.24
  819.0 3.2 copy-start.7
  822.2 1109.9 %reduce-scatter.5.cloned.1.call-start = ((), (), s32[]{:S(2)}) async-start(), calls=%async_computation.8 | async-start | bytes 4259840 | tf_op jit(solution)/shard_map/reduce_scatter | solution.py:137
  841.8 3.5 copy-start.16
  848.0 1.2 copy-start.10
  849.3 1.4 copy-start.11
  900.1 3.5 copy-start.3
  913.5 3.1 copy-start.12
Sparse Core Ops, SparseCore 0:
  9.9 107.4 all-gather.8
  119.2 104.4 all-gather.10
  225.5 104.4 all-gather.6
  331.7 104.4 all-gather.4
  787.4 270.2 reduce-scatter.8
  1060.8 288.5 reduce-scatter.10
  1352.6 288.5 reduce-scatter.6
  1644.4 287.6 reduce-scatter.4
where the time goes:
time: 1970 us; the launch traced here: 1940 us
  waiting for transfers between devices  1690 us (86%)
  local copies, waits for them, and re-layouts  147 us (7%)
  matrix products  53.7 us (3%)
  other arithmetic  32.5 us (2%)
    ppermute x3, waiting for transfers between devices, from_behind(): return lax.ppermute(block, axis, route)  315 us
    reduce_scatter x1, waiting for transfers between devices, shards(): lax.psum_scatter(totals[3], 'dp', scatter_dimension=0, tiled=True)  292 us
    reduce_scatter x1, waiting for transfers between devices, shards(): lax.psum_scatter(totals[1], 'dp', scatter_dimension=0, tiled=True)  292 us
    reduce_scatter x1, waiting for transfers between devices, shards(): lax.psum_scatter(totals[0], 'dp', scatter_dimension=0, tiled=True)  291 us
    reduce_scatter x1, waiting for transfers between devices, shards(): lax.psum_scatter(totals[2], 'dp', scatter_dimension=0, tiled=True)  138 us
    all_gather x1, waiting for transfers between devices, shards(): lax.all_gather(left_dn, 'dp', axis=1, tiled=True)  106 us
    all_gather x1, waiting for transfers between devices, shards(): lax.all_gather(right_dn, 'dp', axis=1, tiled=True)  97.3 us
    all_gather x1, waiting for transfers between devices, shards(): lax.all_gather(right_up, 'dp', axis=1, tiled=True)  82.3 us
  transfers between devices with their start and end apart: 11, of which 11 were waited for; matrix products, arithmetic and copies ran while one was open for 10% of the time, Pallas kernels for 0%

commit v1 on v0

--- a/solution.py
+++ b/solution.py
@@ -8,6 +8,23 @@
 
 epsilon = 1e-06
 
+Z_LO, X, Y, CORE = 2, 4, 4, 2
+EXTENT = {"z": Z_LO, "x": X, "y": Y, "c": CORE}
+STRIDE = {"z": X * Y * CORE, "x": Y * CORE, "y": CORE, "c": 1}
+
+
+def place(axis):
+    return lax.rem(lax.axis_index("dp") // STRIDE[axis], EXTENT[axis])
+
+
+def shifted(block, axis, distance):
+    stride, extent = STRIDE[axis], EXTENT[axis]
+    route = []
+    for device in range(Z_LO * X * Y * CORE):
+        at = device // stride % extent
+        route.append((device, device + ((at + distance) % extent - at) * stride))
+    return lax.ppermute(block, "dp", route)
+
 
 def from_behind(block, axis, distance):
     devices = range(lax.axis_size(axis))
@@ -15,13 +32,64 @@
     return lax.ppermute(block, axis, route)
 
 
+def gather_ring(block, axis):
+    extent = EXTENT[axis]
+    here = place(axis)
+    pieces = [block] + [shifted(block, axis, -d) for d in range(1, extent)]
+    whole = jnp.zeros((extent,) + block.shape, block.dtype)
+    for d, piece in enumerate(pieces):
+        whole = lax.dynamic_update_index_in_dim(whole, piece, lax.rem(here + d, extent), 0)
+    return whole
+
+
+def reduce_ring(block, axis, dim, kind):
+    extent = EXTENT[axis]
+    here = place(axis)
+    total = lax.dynamic_index_in_dim(block, here, dim, keepdims=False).astype(jnp.float32)
+    for d in range(1, extent):
+        piece = lax.dynamic_index_in_dim(block, lax.rem(here + d, extent), dim, keepdims=False)
+        total = total + shifted(piece, axis, d).astype(jnp.float32)
+    return total.astype(kind)
+
+
+def gather_factors(shards_in):
+    packed = jnp.stack(shards_in)
+    packed = gather_ring(packed, "z")
+    first, second = packed[:, :2], packed[:, 2:]
+    first = gather_ring(gather_ring(first, "y"), "x")
+    second = gather_ring(gather_ring(second, "x"), "y")
+    both = jnp.stack([first, second.swapaxes(0, 1)])
+    both = gather_ring(both, "c")
+    both = both.transpose(1, 5, 4, 2, 3, 0, 6, 7)
+    return both.reshape(4, -1, both.shape[-1])
+
+
+def scatter_factors(totals):
+    rows, width = totals[0].shape
+    packed = jnp.stack([t.astype(jnp.bfloat16) for t in totals])
+    packed = packed.reshape(4, Z_LO, X, Y, CORE, -1, width)
+    packed = reduce_ring(packed, "c", 4, jnp.bfloat16)
+    first, second = packed[:2], packed[2:]
+    first = reduce_ring(reduce_ring(first, "x", 2, jnp.bfloat16), "y", 2, jnp.bfloat16)
+    second = reduce_ring(reduce_ring(second, "y", 3, jnp.bfloat16), "x", 2, jnp.bfloat16)
+    return reduce_ring(jnp.concatenate([first, second]), "z", 1, jnp.float32)
+
+
+def contract(form, first, second):
+    return jnp.einsum(form, first, second, preferred_element_type=jnp.float32)
+
+
 def inverse_of(permute):
     count = permute.shape[0]
-    return jnp.zeros((count,), jnp.int32).at[permute].set(jnp.arange(count, dtype=jnp.int32))
-
-
-def contract(form, first, second):
-    return jnp.einsum(form, first, second, preferred_element_type=jnp.float32)
+    return (
+        jnp.zeros((count,), jnp.int32)
+        .at[permute]
+        .set(jnp.arange(count, dtype=jnp.int32), mode="promise_in_bounds", unique_indices=True)
+    )
+
+
+def rows_at(array, index):
+    return array.at[index].get(mode="promise_in_bounds", unique_indices=True)
 
 
 def forward_part(rows_in, weights, tables):
@@ -35,7 +103,7 @@
     normf = in_float * scaling
     normed = normf.astype(jnp.bfloat16).reshape(nblock, width, count)
     up_mid = contract("jio,jit->jot", left_first, normed).astype(jnp.bfloat16).reshape(-1, count)
-    shuffled = jnp.take(up_mid, perm_first, axis=0).reshape(nhidden, narrow, count)
+    shuffled = rows_at(up_mid, perm_first).reshape(nhidden, narrow, count)
     hidden = contract("kio,kit->kot", right_first, shuffled)
     squashed = jax.nn.sigmoid(hidden)
     active = (hidden * squashed).astype(jnp.bfloat16)
@@ -43,7 +111,7 @@
     down_mid = (
         contract("kio,kot->kit", right_second, active).astype(jnp.bfloat16).reshape(-1, count)
     )
-    placed = jnp.take(down_mid, perm_second, axis=0).reshape(nblock, width, count)
+    placed = rows_at(down_mid, perm_second).reshape(nblock, width, count)
     return (scaling, normf, normed, shuffled, active, slope, placed)
 
 
@@ -58,13 +126,13 @@
     grad_placed = (
         contract("jio,jot->jit", left_second, grad_out).astype(jnp.bfloat16).reshape(-1, count)
     )
-    grad_down = jnp.take(grad_placed, inv_second, axis=0).reshape(nhidden, narrow, count)
+    grad_down = rows_at(grad_placed, inv_second).reshape(nhidden, narrow, count)
     grad_active = contract("kio,kit->kot", right_second, grad_down).astype(jnp.bfloat16)
     grad_hidden = (grad_active.astype(jnp.float32) * slope.astype(jnp.float32)).astype(jnp.bfloat16)
     grad_shuffled = (
         contract("kio,kot->kit", right_first, grad_hidden).astype(jnp.bfloat16).reshape(-1, count)
     )
-    grad_upmid = jnp.take(grad_shuffled, inv_first, axis=0).reshape(nblock, width, count)
+    grad_upmid = rows_at(grad_shuffled, inv_first).reshape(nblock, width, count)
     grad_norm = contract("jio,jot->jit", left_first, grad_upmid).reshape(-1, count)
     inner = jnp.mean(grad_norm * normf, axis=0, keepdims=True)
     grad_input = grad_col.astype(jnp.float32) + scaling * (grad_norm - normf * inner)
@@ -72,22 +140,17 @@
 
 
 def shards(acts, cotangent, perm_up, perm_dn, left_up, right_up, right_dn, left_dn):
-    gathered = (
-        lax.all_gather(left_up, "dp", axis=1, tiled=True),
-        lax.all_gather(right_up, "dp", axis=1, tiled=True),
-        lax.all_gather(right_dn, "dp", axis=1, tiled=True),
-        lax.all_gather(left_dn, "dp", axis=1, tiled=True),
-    )
-    model_width = gathered[0].shape[1]
-    width = gathered[0].shape[2]
+    gathered = gather_factors((left_up[0], right_up[0], right_dn[0], left_dn[0]))
+    model_width = gathered.shape[1]
+    width = gathered.shape[2]
     nblock = model_width // width
     nhidden = FF // width
     narrow = model_width // nhidden
     weights = (
-        gathered[0][0].reshape(nblock, width, width),
-        gathered[1][0].reshape(nhidden, narrow, width),
-        gathered[2][0].reshape(nhidden, narrow, width),
-        gathered[3][0].reshape(nblock, width, width),
+        gathered[0].reshape(nblock, width, width),
+        gathered[1].reshape(nhidden, narrow, width),
+        gathered[2].reshape(nhidden, narrow, width),
+        gathered[3].reshape(nblock, width, width),
     )
     tables = (perm_up[0], perm_dn[0], inverse_of(perm_up[0]), inverse_of(perm_dn[0]))
     section_count = lax.axis_size("section")
@@ -133,12 +196,7 @@
         contract("kit,kot->kio", grad_down, active).reshape(-1, width),
         contract("jit,jot->jio", placed, grad_out).reshape(-1, width),
     )
-    owned = (
-        lax.psum_scatter(totals[0], "dp", scatter_dimension=0, tiled=True),
-        lax.psum_scatter(totals[1], "dp", scatter_dimension=0, tiled=True),
-        lax.psum_scatter(totals[2], "dp", scatter_dimension=0, tiled=True),
-        lax.psum_scatter(totals[3], "dp", scatter_dimension=0, tiled=True),
-    )
+    owned = scatter_factors(totals)
     return (results[None], owned[0][None], owned[1][None], owned[2][None], owned[3][None])
 
 

time: 1970 us -> 633 us (0.32)
  waiting for transfers between devices: 1690 us -> 330 us
  starting transfers between devices: 4.66 us -> 54.5 us
  local copies, waits for them, and re-layouts: 147 us -> 167 us
    reduce_scatter x4 -> x0, waiting for transfers between devices: 1010 us -> none  [the longest x1 292 us: shards(): lax.psum_scatter(totals[3], 'dp', scatter_dimension=0, tiled=True)]
    all_gather x4 -> x0, waiting for transfers between devices: 356 us -> none  [the longest x1 106 us: shards(): lax.all_gather(left_dn, 'dp', axis=1, tiled=True)]
    ppermute x0 -> x28, waiting for transfers between devices: none -> 53.5 us  [shifted(): return lax.ppermute(block, 'dp', route)]
    ppermute x0 -> x28, starting transfers between devices: none -> 44.6 us  [shifted(): return lax.ppermute(block, 'dp', route)]
    ppermute x3, waiting for transfers between devices: 315 us -> 276 us  [from_behind(): return lax.ppermute(block, axis, route)]
    select_n x8 -> x1, other arithmetic: 22.3 us -> 0.04 us  [rows_at(): return array.at[index].get(mode='promise_in_bounds', unique_indices=True)]
  transfers between devices with their start and end apart: 11 -> 31, of which waited for: 11 -> 16; matrix products, arithmetic and copies ran while one was open for 10% -> 20% of each run, Pallas kernels for 0% -> 0%
where the time goes in v1:
time: 633 us; the launch traced here: 622 us
  waiting for transfers between devices  330 us (52%)
  local copies, waits for them, and re-layouts  167 us (26%)
  starting transfers between devices  54.5 us (9%)
  matrix products  45.2 us (7%)
  other arithmetic  22 us (3%)
    ppermute x3, waiting for transfers between devices, from_behind(): return lax.ppermute(block, axis, route)  276 us
    gather x6, local copies, waits for them, and re-layouts, rows_at(): return array.at[index].get(mode='promise_in_bounds', unique_indices=True)  90.1 us
    ppermute x28, waiting for transfers between devices, shifted(): return lax.ppermute(block, 'dp', route)  53.5 us
    dot_general x13, matrix products, contract(): return jnp.einsum(form, first, second, preferred_element_type=jnp.float32)  45.2 us
    ppermute x28, starting transfers between devices, shifted(): return lax.ppermute(block, 'dp', route)  44.6 us
    scatter x2, local copies, waits for them, and re-layouts, inverse_of(): return jnp.zeros((count,), jnp.int32).at[permute].set(jnp.arange(count, d...  31.1 us
  transfers between devices with their start and end apart: 31, of which 16 were waited for; matrix products, arithmetic and copies ran while one was open for 20% of the time, Pallas kernels for 0%

profile of v1, /device:TPU:6, one launch (start us, length us, event | category | flops | bytes accessed | tf_op | source)
XLA Modules:
  0.0 621.5 jit_solution(17104148463937553642)
XLA Ops:
  3.7 1.9 collective-permute-start
  5.6 3.4 collective-permute-done
  10.0 2.4 collective-permute-start.8
  13.2 3.0 collective-permute-start.1
  17.8 1.6 collective-permute-start.3
  19.4 2.0 collective-permute-start.10
  21.5 1.7 collective-permute-start.11
  23.9 10.9 %collective-permute-done.3 = bf16[2,2,64,256]{3,2,1,0:T(8,128)(2,1)S(1)} collective-permute-done((bf16[2,2,64,256]{3,2,1,0:T(8,128)(2,1)S(1)}, bf16[2,2,64,256]{3,2,1,0:T(8,128)(2,1)S(1)}, u32[]{:S(2)}, u32[]{:S(2)}) %collective-permute-start.3) | collective-permute-done | bytes 131104 | tf_op jit(solution)/shard_map/ppermute | solution.py:26
  34.9 3.6 collective-permute-start.5
  39.2 3.7 collective-permute-done.10
  42.9 2.9 collective-permute-start.6
  46.7 4.5 collective-permute-done.5
  52.6 3.6 pad_maximum_fusion.1
  58.2 2.3 copy.176
  60.6 15.5 %scatter_custom_fusion = s32[4096]{0:T(1024)S(1)} fusion(s32[4096]{0:T(1024)S(1)} %bitcast.384, s32[4096]{0:T(1024)S(1)} %iota.6, s32[]{:T(128)} %constant.249.clone.1), kind=kCustom, calls=%fused_computation.182 | custom fusion | bytes 16388 | tf_op jit(solution)/shard_map/scatter | solution.py:87
  76.1 15.5 %scatter_custom_fusion.1 = s32[4096]{0:T(1024)S(1)} fusion(s32[4096]{0:T(1024)S(1)} %bitcast.386, s32[4096]{0:T(1024)S(1)} %iota.7, s32[]{:T(128)} %constant.249.clone.1), kind=kCustom, calls=%fused_computation.180 | custom fusion | bytes 16388 | tf_op jit(solution)/shard_map/scatter | solution.py:87
  94.5 2.8 copy_dynamic-update-slice_fusion
  97.3 2.7 fusion.81
  101.4 15.0 %gather_fusion.8 = bf16[4096,128]{1,0:T(8,128)(2,1)} fusion(bf16[4096,128]{1,0:T(8,128)(2,1)S(1)} %bitcast.326, s32[4096]{0:T(1024)S(1)} %broadcast_clamp_fusion.1), kind=kCustom, calls=%fused_computation.8 | custom fusion | bytes 2113536 | tf_op jit(solution)/shard_map/gather | solution.py:92
  116.4 9.4 %multiply_convert_fusion = (bf16[64,256,128]{2,1,0:T(8,128)(2,1)}, bf16[64,256,128]{2,1,0:T(8,128)(2,1)}) fusion(bf16[64,64,256]{2,1,0:T(8,128)(2,1)} %bitcast.328, bf16[64,64,128]{2,1,0:T(8,128)(2,1)} %bitcast.365), kind=kOutput, calls=%fused_computation.89 | convolution fusion | flops 289406976 | bytes 11534336 | tf_op jit(solution)/shard_map/kio,kit->kot/dot_general | solution.py:79
  128.4 50.4 %collective-permute-done.14 = bf16[2,64,4096]{2,1,0:T(8,128)(2,1)S(1)} collective-permute-done((bf16[2,64,4096]{2,1,0:T(8,128)(2,1)}, bf16[2,64,4096]{2,1,0:T(8,128)(2,1)S(1)}, u32[]{:S(2)}, u32[]{:S(2)}) %collective-permute-start.14) | collective-permute-done | bytes 1048608 | tf_op jit(solution)/shard_map/ppermute | solution.py:32
  180.6 46.9 %collective-permute-done.15 = bf16[2,64,4096]{2,1,0:T(8,128)(2,1)S(1)} collective-permute-done((bf16[2,64,4096]{2,1,0:T(8,128)(2,1)}, bf16[2,64,4096]{2,1,0:T(8,128)(2,1)S(1)}, u32[]{:S(2)}, u32[]{:S(2)}) %collective-permute-start.15) | collective-permute-done | bytes 1048608 | tf_op jit(solution)/shard_map/ppermute | solution.py:32
  227.7 7.4 %collective-permute-start.16 = (bf16[2,64,4096]{2,1,0:T(8,128)(2,1)}, bf16[2,64,4096]{2,1,0:T(8,128)(2,1)}, u32[]{:S(2)}, u32[]{:S(2)}) collective-permute-start(bf16[2,64,4096]{2,1,0:T(8,128)(2,1)} %get-tuple-element.344), channel_id=1, source_target_pairs={{64,0},{128,64},{192,128},{65,1},{129,65},{193,129},{66,2},{130,66... | collective-permute-start | bytes 3145736 | tf_op jit(solution)/shard_map/ppermute | solution.py:32
  235.1 3.7 convolution_convert_fusion.8
  238.8 15.0 %gather_fusion.11 = bf16[4096,128]{1,0:T(8,128)(2,1)} fusion(bf16[4096,128]{1,0:T(8,128)(2,1)S(1)} %bitcast.321, s32[4096]{0:T(1024)S(1)} %broadcast_clamp_fusion), kind=kCustom, calls=%fused_computation.11 | custom fusion | bytes 2113536 | tf_op jit(solution)/shard_map/gather | solution.py:92
  253.8 178.9 %collective-permute-done.16 = bf16[2,64,4096]{2,1,0:T(8,128)(2,1)} collective-permute-done((bf16[2,64,4096]{2,1,0:T(8,128)(2,1)}, bf16[2,64,4096]{2,1,0:T(8,128)(2,1)}, u32[]{:S(2)}, u32[]{:S(2)}) %collective-permute-start.16) | collective-permute-done | bytes 1048608 | tf_op jit(solution)/shard_map/ppermute | solution.py:32
  434.1 1.4 copy.177
  435.5 2.5 convolution_convert_fusion.10
  438.1 15.0 %gather_fusion.9 = bf16[4096,128]{1,0:T(8,128)(2,1)} fusion(bf16[4096,128]{1,0:T(8,128)(2,1)S(1)} %bitcast.327, s32[4096]{0:T(1024)S(1)} %fusion.72), kind=kCustom, calls=%fused_computation.9 | custom fusion | bytes 2113536 | tf_op jit(solution)/shard_map/gather | solution.py:92
  453.1 5.5 convolution_convert_fusion.4
  458.6 1.8 multiply_convert_fusion.1
  460.5 3.0 convolution_convert_fusion.5
  465.0 2.1 convolution_convert_fusion.6
  467.1 15.0 %gather_fusion.10 = bf16[4096,128]{1,0:T(8,128)(2,1)} fusion(bf16[4096,128]{1,0:T(8,128)(2,1)S(1)} %bitcast.316, s32[4096]{0:T(1024)S(1)} %fusion.73), kind=kCustom, calls=%fused_computation.10 | custom fusion | bytes 2113536 | tf_op jit(solution)/shard_map/gather | solution.py:92
  482.1 2.4 convolution_convert_fusion.7
  484.9 3.0 pad_maximum_fusion
  487.9 4.2 constant_dynamic-slice_fusion.1
  492.1 2.7 copy.201
  495.1 7.1 %collective-permute-done.17 = bf16[4,2,4,4,64,256]{5,4,0,1,2,3:T(8,128)(2,1)S(1)} collective-permute-done((bf16[4,2,4,4,64,256]{5,4,0,1,2,3:T(8,128)(2,1)S(1)}, bf16[4,2,4,4,64,256]{5,4,0,1,2,3:T(8,128)(2,1)S(1)}, u32[]{:S(2)}, u32[]{:S(2)}) %collective-permute-start.17) | collective-permute-done | bytes 4194336 | tf_op jit(solution)/shard_map/ppermute | solution.py:26
  502.3 2.2 fusion.53
  506.0 1.6 collective-permute-start.20
  507.6 3.1 collective-permute-start.19
  512.0 3.5 collective-permute-start.26
  515.5 5.9 collective-permute-done.20
  522.2 11.7 %collective-permute-done.19 = bf16[2,2,4,64,256]{4,3,0,1,2:T(8,128)(2,1)} collective-permute-done((bf16[2,2,4,64,256]{4,3,0,1,2:T(8,128)(2,1)}, bf16[2,2,4,64,256]{4,3,0,1,2:T(8,128)(2,1)}, u32[]{:S(2)}, u32[]{:S(2)}) %collective-permute-start.19) | collective-permute-done | bytes 524320 | tf_op jit(solution)/shard_map/ppermute | solution.py:26
  533.9 1.9 fusion.61
  535.8 3.8 collective-permute-start.23
  541.7 1.9 fusion.58
  543.6 1.8 collective-permute-start.29
  545.4 4.1 collective-permute-start.28
  549.5 2.5 collective-permute-start.27
  552.1 1.6 collective-permute-done.28
  555.6 63.8 %conditional.7 = (bf16[1,2,64,4096]{3,2,1,0:T(8,128)(2,1)}) conditional(s32[]{:T(128)} %convert_element_type.325, bf16[2,64,4096]{2,1,0:T(8,128)(2,1)} %get-tuple-element.344, (bf16[2,64,4096]{2,1,0:T(8,128)(2,1)S(1)}, f32[1,128]{1,0:T(1,128)S(1)}, bf16[16,256,256]{2,1,0:T(8,128)(2,1)}, s32[4096]{0:T(1024)S(1)}, bf16[64,64,256]{2,1,0:T(8,128)(2,1)}, ...), branch_computations={%region_12.13_spmd, %region_13.15_spmd} | conditional | flops 1089503232 | bytes 74549856 | solution.py:181
  555.6 6.8 %copy.157 = bf16[64,256,128]{1,2,0:T(8,128)(2,1)} copy(bf16[64,256,128]{2,1,0:T(8,128)(2,1)} %get-tuple-element.293) | data formatting | bytes 8388608 | tf_op jit(solution)/shard_map
  563.7 2.5 convolution_convert_fusion.3
  566.3 15.0 %gather_fusion.6 = bf16[4096,128]{1,0:T(8,128)(2,1)} fusion(bf16[4096,128]{1,0:T(8,128)(2,1)S(1)} %bitcast.325, s32[4096]{0:T(1024)S(1)} %get-tuple-element.304), kind=kCustom, calls=%fused_computation.6 | custom fusion | bytes 2113536 | tf_op jit(solution)/shard_map/cond/branch_1_fun/gather | solution.py:92
  581.3 6.5 %fusion.48 = bf16[64,128,64]{1,2,0:T(8,128)(2,1)S(1)} fusion(bf16[64,64,256]{2,1,0:T(8,128)(2,1)} %get-tuple-element.133, bf16[64,256,128]{1,2,0:T(8,128)(2,1)} %copy.157, bf16[64,64,128]{2,1,0:T(8,128)(2,1)} %bitcast.370, bf16[64,64,256]{2,1,0:T(8,128)(2,1)} %get-tuple-element.131), kind=kOutput, calls=%fused_computation.80 | convolution fusion | flops 547880960 | bytes 10485760 | tf_op jit(solution)/shard_map/cond/branch_1_fun/kio,kot->kit/dot_general | solution.py:79
  587.8 15.0 %gather_fusion.7 = bf16[4096,128]{1,0:T(8,128)(2,1)} fusion(bf16[4096,128]{1,0:T(8,128)(2,1)S(1)} %bitcast.320, s32[4096]{0:T(1024)S(1)} %get-tuple-element.305), kind=kCustom, calls=%fused_computation.7 | custom fusion | bytes 2113536 | tf_op jit(solution)/shard_map/cond/branch_1_fun/gather | solution.py:92
  602.8 4.1 convolution_bitcast_fusion.3
  606.9 3.0 copy.143
  609.9 2.9 copy.145
  612.8 1.8 copy.144
  614.6 2.9 multiply_reduce_fusion.3
  617.8 1.6 add_convert_fusion.3
  (147 shorter events, 35.3 us)
Async XLA Ops:
  3.7 5.4 collective-permute-start
  9.1 8.7 %collective-permute-start.7 = (bf16[2,2,64,256]{3,2,1,0:T(8,128)(2,1)S(1)}, bf16[2,2,64,256]{3,2,1,0:T(8,128)(2,1)S(1)}, u32[]{:S(2)}, u32[]{:S(2)}) collective-permute-start(bf16[2,2,64,256]{3,2,1,0:T(8,128)(2,1)S(1)} %get-tuple-element.337), channel_id=1, source_target_pairs={{0,24},{1,25},{2,26},{3,27},{4,28},{5,29},{6,30},{7,31},{8,0},{9,1... | collective-permute-start | bytes 393224 | tf_op jit(solution)/shard_map/ppermute | solution.py:26
  10.0 9.3 %collective-permute-start.8 = (bf16[2,2,64,256]{3,2,1,0:T(8,128)(2,1)S(1)}, bf16[2,2,64,256]{3,2,1,0:T(8,128)(2,1)S(1)}, u32[]{:S(2)}, u32[]{:S(2)}) collective-permute-start(bf16[2,2,64,256]{3,2,1,0:T(8,128)(2,1)S(1)} %get-tuple-element.337), channel_id=1, source_target_pairs={{0,16},{1,17},{2,18},{3,19},{4,20},{5,21},{6,22},{7,23},{8,24},{9,... | collective-permute-start | bytes 393224 | tf_op jit(solution)/shard_map/ppermute | solution.py:26
  12.4 7.0 %collective-permute-start.9 = (bf16[2,2,64,256]{3,2,1,0:T(8,128)(2,1)S(1)}, bf16[2,2,64,256]{3,2,1,0:T(8,128)(2,1)S(1)}, u32[]{:S(2)}, u32[]{:S(2)}) collective-permute-start(bf16[2,2,64,256]{3,2,1,0:T(8,128)(2,1)S(1)} %get-tuple-element.337), channel_id=1, source_target_pairs={{0,8},{1,9},{2,10},{3,11},{4,12},{5,13},{6,14},{7,15},{8,16},{9,17... | collective-permute-start | bytes 393224 | tf_op jit(solution)/shard_map/ppermute | solution.py:26
  13.2 9.9 %collective-permute-start.1 = (bf16[2,2,64,256]{3,2,1,0:T(8,128)(2,1)S(1)}, bf16[2,2,64,256]{3,2,1,0:T(8,128)(2,1)S(1)}, u32[]{:S(2)}, u32[]{:S(2)}) collective-permute-start(bf16[2,2,64,256]{3,2,1,0:T(8,128)(2,1)S(1)} %get-tuple-element.336), channel_id=1, source_target_pairs={{0,6},{1,7},{2,0},{3,1},{4,2},{5,3},{6,4},{7,5},{8,14},{9,15},{10,... | collective-permute-start | bytes 393224 | tf_op jit(solution)/shard_map/ppermute | solution.py:26
  16.3 7.6 %collective-permute-start.2 = (bf16[2,2,64,256]{3,2,1,0:T(8,128)(2,1)S(1)}, bf16[2,2,64,256]{3,2,1,0:T(8,128)(2,1)S(1)}, u32[]{:S(2)}, u32[]{:S(2)}) collective-permute-start(bf16[2,2,64,256]{3,2,1,0:T(8,128)(2,1)S(1)} %get-tuple-element.336), channel_id=1, source_target_pairs={{0,4},{1,5},{2,6},{3,7},{4,0},{5,1},{6,2},{7,3},{8,12},{9,13},{10,... | collective-permute-start | bytes 393224 | tf_op jit(solution)/shard_map/ppermute | solution.py:26
  17.8 17.0 %collective-permute-start.3 = (bf16[2,2,64,256]{3,2,1,0:T(8,128)(2,1)S(1)}, bf16[2,2,64,256]{3,2,1,0:T(8,128)(2,1)S(1)}, u32[]{:S(2)}, u32[]{:S(2)}) collective-permute-start(bf16[2,2,64,256]{3,2,1,0:T(8,128)(2,1)S(1)} %get-tuple-element.336), channel_id=1, source_target_pairs={{0,2},{1,3},{2,4},{3,5},{4,6},{5,7},{6,0},{7,1},{8,10},{9,11},{10,... | collective-permute-start | bytes 393224 | tf_op jit(solution)/shard_map/ppermute | solution.py:26
  19.4 23.5 %collective-permute-start.10 = (bf16[4,2,2,64,256]{4,3,2,1,0:T(8,128)(2,1)S(1)}, bf16[4,2,2,64,256]{4,3,2,1,0:T(8,128)(2,1)S(1)}, u32[]{:S(2)}, u32[]{:S(2)}) collective-permute-start(bf16[4,2,2,64,256]{4,3,2,1,0:T(8,128)(2,1)S(1)} %bitcast_dynamic-update-slice_fusion.8), channel_id=1, source_target_pairs={{0,6},{1,7},{2,0},{3,1},{4,2},{5,3},{6,4},{7,5},{8,14},{9,15},{10,... | collective-permute-start | bytes 1572872 | tf_op jit(solution)/shard_map/ppermute | solution.py:26
  21.5 24.4 %collective-permute-start.11 = (bf16[4,2,2,64,256]{4,3,2,1,0:T(8,128)(2,1)S(1)}, bf16[4,2,2,64,256]{4,3,2,1,0:T(8,128)(2,1)S(1)}, u32[]{:S(2)}, u32[]{:S(2)}) collective-permute-start(bf16[4,2,2,64,256]{4,3,2,1,0:T(8,128)(2,1)S(1)} %bitcast_dynamic-update-slice_fusion.8), channel_id=1, source_target_pairs={{0,4},{1,5},{2,6},{3,7},{4,0},{5,1},{6,2},{7,3},{8,12},{9,13},{10,... | collective-permute-start | bytes 1572872 | tf_op jit(solution)/shard_map/ppermute | solution.py:26
  23.2 23.4 %collective-permute-start.12 = (bf16[4,2,2,64,256]{4,3,2,1,0:T(8,128)(2,1)S(1)}, bf16[4,2,2,64,256]{4,3,2,1,0:T(8,128)(2,1)S(1)}, u32[]{:S(2)}, u32[]{:S(2)}) collective-permute-start(bf16[4,2,2,64,256]{4,3,2,1,0:T(8,128)(2,1)S(1)} %bitcast_dynamic-update-slice_fusion.8), channel_id=1, source_target_pairs={{0,2},{1,3},{2,4},{3,5},{4,6},{5,7},{6,0},{7,1},{8,10},{9,11},{10,... | collective-permute-start | bytes 1572872 | tf_op jit(solution)/shard_map/ppermute | solution.py:26
  34.8 11.8 %collective-permute-start.4 = (bf16[4,2,2,64,256]{4,3,2,1,0:T(8,128)(2,1)S(1)}, bf16[4,2,2,64,256]{4,3,2,1,0:T(8,128)(2,1)S(1)}, u32[]{:S(2)}, u32[]{:S(2)}) collective-permute-start(bf16[4,2,2,64,256]{4,3,2,1,0:T(8,128)(2,1)S(1)} %bitcast_dynamic-update-slice_fusion.12), channel_id=1, source_target_pairs={{0,24},{1,25},{2,26},{3,27},{4,28},{5,29},{6,30},{7,31},{8,0},{9,1... | collective-permute-start | bytes 1572872 | tf_op jit(solution)/shard_map/ppermute | solution.py:26
  34.9 16.3 %collective-permute-start.5 = (bf16[4,2,2,64,256]{4,3,2,1,0:T(8,128)(2,1)S(1)}, bf16[4,2,2,64,256]{4,3,2,1,0:T(8,128)(2,1)S(1)}, u32[]{:S(2)}, u32[]{:S(2)}) collective-permute-start(bf16[4,2,2,64,256]{4,3,2,1,0:T(8,128)(2,1)S(1)} %bitcast_dynamic-update-slice_fusion.12), channel_id=1, source_target_pairs={{0,16},{1,17},{2,18},{3,19},{4,20},{5,21},{6,22},{7,23},{8,24},{9,... | collective-permute-start | bytes 1572872 | tf_op jit(solution)/shard_map/ppermute | solution.py:26
  42.9 9.6 %collective-permute-start.6 = (bf16[4,2,2,64,256]{4,3,2,1,0:T(8,128)(2,1)S(1)}, bf16[4,2,2,64,256]{4,3,2,1,0:T(8,128)(2,1)S(1)}, u32[]{:S(2)}, u32[]{:S(2)}) collective-permute-start(bf16[4,2,2,64,256]{4,3,2,1,0:T(8,128)(2,1)S(1)} %bitcast_dynamic-update-slice_fusion.12), channel_id=1, source_target_pairs={{0,8},{1,9},{2,10},{3,11},{4,12},{5,13},{6,14},{7,15},{8,16},{9,17... | collective-permute-start | bytes 1572872 | tf_op jit(solution)/shard_map/ppermute | solution.py:26
  52.6 3.9 copy-start.34
  56.2 38.3 %collective-permute-start.13 = (bf16[2,4,4,2,2,64,256]{6,5,4,3,2,1,0:T(8,128)(2,1)}, bf16[2,4,4,2,2,64,256]{6,5,4,3,2,1,0:T(8,128)(2,1)}, u32[]{:S(2)}, u32[]{:S(2)}) collective-permute-start(bf16[2,4,4,2,2,64,256]{6,5,4,3,2,1,0:T(8,128)(2,1)} %get-tuple-element.316), channel_id=1, source_target_pairs={{0,1},{1,0},{2,3},{3,2},{4,5},{5,4},{6,7},{7,6},{8,9},{9,8},{10,11... | collective-permute-start | bytes 12582920 | tf_op jit(solution)/shard_map/ppermute | solution.py:26
  58.2 2.3 copy-start.40
  58.2 2.3 copy-start.41
  91.7 2.2 copy-start.7
  97.3 2.7 copy-start.17
  100.0 1.4 copy-start.3
  116.4 9.4 %copy-start.9 = (bf16[2,64,4096]{2,1,0:T(8,128)(2,1)S(1)}, bf16[2,64,4096]{2,1,0:T(8,128)(2,1)}, u32[]{:S(2)}) copy-start(bf16[2,64,4096]{2,1,0:T(8,128)(2,1)} %param.17) | copy-start | bytes 3145732
  126.1 1.0 copy-start.38
  127.1 51.7 %collective-permute-start.14 = (bf16[2,64,4096]{2,1,0:T(8,128)(2,1)}, bf16[2,64,4096]{2,1,0:T(8,128)(2,1)S(1)}, u32[]{:S(2)}, u32[]{:S(2)}) collective-permute-start(bf16[2,64,4096]{2,1,0:T(8,128)(2,1)} %copy-done.38), channel_id=1, source_target_pairs={{64,0},{128,64},{192,128},{65,1},{129,65},{193,129},{66,2},{130,66... | collective-permute-start | bytes 3145736 | tf_op jit(solution)/shard_map/ppermute | solution.py:32
  179.3 48.2 %collective-permute-start.15 = (bf16[2,64,4096]{2,1,0:T(8,128)(2,1)}, bf16[2,64,4096]{2,1,0:T(8,128)(2,1)S(1)}, u32[]{:S(2)}, u32[]{:S(2)}) collective-permute-start(bf16[2,64,4096]{2,1,0:T(8,128)(2,1)} %get-tuple-element.343), channel_id=1, source_target_pairs={{64,0},{128,64},{192,128},{65,1},{129,65},{193,129},{66,2},{130,66... | collective-permute-start | bytes 3145736 | tf_op jit(solution)/shard_map/ppermute | solution.py:32
  227.7 205.1 %collective-permute-start.16 = (bf16[2,64,4096]{2,1,0:T(8,128)(2,1)}, bf16[2,64,4096]{2,1,0:T(8,128)(2,1)}, u32[]{:S(2)}, u32[]{:S(2)}) collective-permute-start(bf16[2,64,4096]{2,1,0:T(8,128)(2,1)} %get-tuple-element.344), channel_id=1, source_target_pairs={{64,0},{128,64},{192,128},{65,1},{129,65},{193,129},{66,2},{130,66... | collective-permute-start | bytes 3145736 | tf_op jit(solution)/shard_map/ppermute | solution.py:32
  434.1 1.4 copy-start.12
  453.1 5.5 copy-start
  453.1 5.5 copy-start.1
  453.1 5.5 copy-start.16
  458.6 1.8 copy-start.33
  460.4 3.0 copy-start.2
  463.5 1.2 copy-start.22
  463.5 1.5 copy-start.35
  482.1 2.4 copy-start.31
  482.1 2.9 copy-start.32
  492.1 10.2 %copy-start.8 = (bf16[4,2,4,4,1,64,256]{6,5,4,3,2,1,0:T(8,128)(2,1)S(1)}, bf16[4,2,4,4,1,64,256]{6,5,4,3,2,1,0:T(8,128)(2,1)}, u32[]{:S(2)}) copy-start(bf16[4,2,4,4,1,64,256]{6,5,4,3,2,1,0:T(8,128)(2,1)} %get-tuple-element.306) | copy-start | bytes 12582916
  494.8 7.5 %collective-permute-start.17 = (bf16[4,2,4,4,64,256]{5,4,0,1,2,3:T(8,128)(2,1)S(1)}, bf16[4,2,4,4,64,256]{5,4,0,1,2,3:T(8,128)(2,1)S(1)}, u32[]{:S(2)}, u32[]{:S(2)}) collective-permute-start(bf16[4,2,4,4,64,256]{5,4,0,1,2,3:T(8,128)(2,1)S(1)} %bitcast.375), channel_id=1, source_target_pairs={{0,1},{1,0},{2,3},{3,2},{4,5},{5,4},{6,7},{7,6},{8,9},{9,8},{10,11... | collective-permute-start | bytes 12582920 | tf_op jit(solution)/shard_map/ppermute | solution.py:26
  504.8 7.2 %copy-start.29 = (bf16[2,2,4,4,64,256]{5,4,0,1,2,3:T(8,128)(2,1)}, bf16[2,2,4,4,64,256]{5,4,0,1,2,3:T(8,128)(2,1)S(1)}, u32[]{:S(2)}) copy-start(bf16[2,2,4,4,64,256]{5,4,0,1,2,3:T(8,128)(2,1)S(1)} %get-tuple-element.314) | copy-start | bytes 6291460
  504.8 7.2 %copy-start.30 = (bf16[2,2,4,4,64,256]{5,4,0,1,2,3:T(8,128)(2,1)}, bf16[2,2,4,4,64,256]{5,4,0,1,2,3:T(8,128)(2,1)S(1)}, u32[]{:S(2)}) copy-start(bf16[2,2,4,4,64,256]{5,4,0,1,2,3:T(8,128)(2,1)S(1)} %get-tuple-element.315) | copy-start | bytes 6291460
  506.0 15.4 %collective-permute-start.20 = (bf16[2,2,4,64,256]{4,3,0,1,2:T(8,128)(2,1)S(1)}, bf16[2,2,4,64,256]{4,3,0,1,2:T(8,128)(2,1)S(1)}, u32[]{:S(2)}, u32[]{:S(2)}) collective-permute-start(bf16[2,2,4,64,256]{4,3,0,1,2:T(8,128)(2,1)S(1)} %get-tuple-element.322), channel_id=1, source_target_pairs={{0,24},{1,25},{2,26},{3,27},{4,28},{5,29},{6,30},{7,31},{8,0},{9,1... | collective-permute-start | bytes 1572872 | tf_op jit(solution)/shard_map/ppermute | solution.py:26
  507.6 26.3 %collective-permute-start.19 = (bf16[2,2,4,64,256]{4,3,0,1,2:T(8,128)(2,1)}, bf16[2,2,4,64,256]{4,3,0,1,2:T(8,128)(2,1)}, u32[]{:S(2)}, u32[]{:S(2)}) collective-permute-start(bf16[2,2,4,64,256]{4,3,0,1,2:T(8,128)(2,1)} %get-tuple-element.323), channel_id=1, source_target_pairs={{0,16},{1,17},{2,18},{3,19},{4,20},{5,21},{6,22},{7,23},{8,24},{9,... | collective-permute-start | bytes 1572872 | tf_op jit(solution)/shard_map/ppermute | solution.py:26
  510.6 23.3 %collective-permute-start.18 = (bf16[2,2,4,64,256]{4,3,0,1,2:T(8,128)(2,1)S(1)}, bf16[2,2,4,64,256]{4,3,0,1,2:T(8,128)(2,1)}, u32[]{:S(2)}, u32[]{:S(2)}) collective-permute-start(bf16[2,2,4,64,256]{4,3,0,1,2:T(8,128)(2,1)S(1)} %get-tuple-element.321), channel_id=1, source_target_pairs={{0,8},{1,9},{2,10},{3,11},{4,12},{5,13},{6,14},{7,15},{8,16},{9,17... | collective-permute-start | bytes 1572872 | tf_op jit(solution)/shard_map/ppermute | solution.py:26
  512.0 27.6 %collective-permute-start.26 = (bf16[2,2,4,64,256]{4,3,0,1,2:T(8,128)(2,1)S(1)}, bf16[2,2,4,64,256]{4,3,0,1,2:T(8,128)(2,1)}, u32[]{:S(2)}, u32[]{:S(2)}) collective-permute-start(bf16[2,2,4,64,256]{4,3,0,1,2:T(8,128)(2,1)S(1)} %get-tuple-element.319), channel_id=1, source_target_pairs={{0,6},{1,7},{2,0},{3,1},{4,2},{5,3},{6,4},{7,5},{8,14},{9,15},{10,... | collective-permute-start | bytes 1572872 | tf_op jit(solution)/shard_map/ppermute | solution.py:26
  515.5 25.1 %collective-permute-start.25 = (bf16[2,2,4,64,256]{4,3,0,1,2:T(8,128)(2,1)}, bf16[2,2,4,64,256]{4,3,0,1,2:T(8,128)(2,1)}, u32[]{:S(2)}, u32[]{:S(2)}) collective-permute-start(bf16[2,2,4,64,256]{4,3,0,1,2:T(8,128)(2,1)} %get-tuple-element.320), channel_id=1, source_target_pairs={{0,4},{1,5},{2,6},{3,7},{4,0},{5,1},{6,2},{7,3},{8,12},{9,13},{10,... | collective-permute-start | bytes 1572872 | tf_op jit(solution)/shard_map/ppermute | solution.py:26
  521.4 0.8 copy-start.39
  522.2 19.5 %collective-permute-start.24 = (bf16[2,2,4,64,256]{4,3,0,1,2:T(8,128)(2,1)}, bf16[2,2,4,64,256]{4,3,0,1,2:T(8,128)(2,1)}, u32[]{:S(2)}, u32[]{:S(2)}) collective-permute-start(bf16[2,2,4,64,256]{4,3,0,1,2:T(8,128)(2,1)} %get-tuple-element.318), channel_id=1, source_target_pairs={{0,2},{1,3},{2,4},{3,5},{4,6},{5,7},{6,0},{7,1},{8,10},{9,11},{10,... | collective-permute-start | bytes 1572872 | tf_op jit(solution)/shard_map/ppermute | solution.py:26
  535.8 13.6 %collective-permute-start.23 = (bf16[2,2,64,256]{3,2,0,1:T(8,128)(2,1)S(1)}, bf16[2,2,64,256]{3,2,0,1:T(8,128)(2,1)S(1)}, u32[]{:S(2)}, u32[]{:S(2)}) collective-permute-start(bf16[2,2,64,256]{3,2,0,1:T(8,128)(2,1)S(1)} %get-tuple-element.330), channel_id=1, source_target_pairs={{0,6},{1,7},{2,0},{3,1},{4,2},{5,3},{6,4},{7,5},{8,14},{9,15},{10,... | collective-permute-start | bytes 393224 | tf_op jit(solution)/shard_map/ppermute | solution.py:26
  539.6 12.4 %collective-permute-start.22 = (bf16[2,2,64,256]{3,2,0,1:T(8,128)(2,1)S(1)}, bf16[2,2,64,256]{3,2,0,1:T(8,128)(2,1)S(1)}, u32[]{:S(2)}, u32[]{:S(2)}) collective-permute-start(bf16[2,2,64,256]{3,2,0,1:T(8,128)(2,1)S(1)} %get-tuple-element.331), channel_id=1, source_target_pairs={{0,4},{1,5},{2,6},{3,7},{4,0},{5,1},{6,2},{7,3},{8,12},{9,13},{10,... | collective-permute-start | bytes 393224 | tf_op jit(solution)/shard_map/ppermute | solution.py:26
  539.6 16.0 %copy-start.13 = (bf16[2,64,4096]{2,1,0:T(8,128)(2,1)S(1)}, bf16[2,64,4096]{2,1,0:T(8,128)(2,1)}, u32[]{:S(2)}) copy-start(bf16[2,64,4096]{2,1,0:T(8,128)(2,1)} %copy-done.12) | copy-start | bytes 3145732
  539.6 12.4 %collective-permute-start.21 = (bf16[2,2,64,256]{3,2,0,1:T(8,128)(2,1)S(1)}, bf16[2,2,64,256]{3,2,0,1:T(8,128)(2,1)S(1)}, u32[]{:S(2)}, u32[]{:S(2)}) collective-permute-start(bf16[2,2,64,256]{3,2,0,1:T(8,128)(2,1)S(1)} %get-tuple-element.329), channel_id=1, source_target_pairs={{0,2},{1,3},{2,4},{3,5},{4,6},{5,7},{6,0},{7,1},{8,10},{9,11},{10,... | collective-permute-start | bytes 393224 | tf_op jit(solution)/shard_map/ppermute | solution.py:26
  543.6 8.5 %collective-permute-start.29 = (bf16[2,2,64,256]{3,2,0,1:T(8,128)(2,1)S(1)}, bf16[2,2,64,256]{3,2,0,1:T(8,128)(2,1)S(1)}, u32[]{:S(2)}, u32[]{:S(2)}) collective-permute-start(bf16[2,2,64,256]{3,2,0,1:T(8,128)(2,1)S(1)} %get-tuple-element.327), channel_id=1, source_target_pairs={{0,24},{1,25},{2,26},{3,27},{4,28},{5,29},{6,30},{7,31},{8,0},{9,1... | collective-permute-start | bytes 393224 | tf_op jit(solution)/shard_map/ppermute | solution.py:26
  545.4 8.3 %collective-permute-start.28 = (bf16[2,2,64,256]{3,2,0,1:T(8,128)(2,1)S(1)}, bf16[2,2,64,256]{3,2,0,1:T(8,128)(2,1)S(1)}, u32[]{:S(2)}, u32[]{:S(2)}) collective-permute-start(bf16[2,2,64,256]{3,2,0,1:T(8,128)(2,1)S(1)} %get-tuple-element.328), channel_id=1, source_target_pairs={{0,16},{1,17},{2,18},{3,19},{4,20},{5,21},{6,22},{7,23},{8,24},{9,... | collective-permute-start | bytes 393224 | tf_op jit(solution)/shard_map/ppermute | solution.py:26
  549.5 5.1 collective-permute-start.27
  555.3 64.1 %collective-permute-start.30 = (bf16[4,64,256]{2,1,0:T(8,128)(2,1)}, bf16[4,64,256]{2,1,0:T(8,128)(2,1)}, u32[]{:S(2)}, u32[]{:S(2)}) collective-permute-start(bf16[4,64,256]{2,1,0:T(8,128)(2,1)} %fusion.69), channel_id=1, source_target_pairs={{0,32},{1,33},{2,34},{3,35},{4,36},{5,37},{6,38},{7,39},{8,40},{9,... | collective-permute-start | bytes 393224 | tf_op jit(solution)/shard_map/ppermute | solution.py:26
  555.6 6.8 %copy-start.14 = (bf16[2,64,4096]{2,1,0:T(8,128)(2,1)}, bf16[2,64,4096]{2,1,0:T(8,128)(2,1)S(1)}, u32[]{:S(2)}) copy-start(bf16[2,64,4096]{2,1,0:T(8,128)(2,1)S(1)} %get-tuple-element.127) | copy-start | bytes 3145732 | tf_op jit(solution)/shard_map/cond
  614.6 2.9 copy-start.15
  614.6 3.2 copy-start.28
